TPU v7x, 256 devices: a whole 4x4x8 slice. The times are simulated.
256 devices in a mesh: img: 8 (over y, core), txt: 32 (over x, z).
Axes of the slice: x: 4, y: 4, z: 8, core: 2. Of those that a mesh axis runs over, the one named last changes fastest.
Arguments:
- picture_embeddings: bfloat16 [16384, 1152], P(('img', 'txt')), may hold values from -4 to 4
- caption_embeddings: bfloat16 [16384, 1152], P(('txt', 'img')), may hold values from -4 to 4
- sharpness_factor: float32 [1], replicated, may hold values from 24 to 32
- pairing_shift: float32 [1], replicated, may hold values from -7 to -5
Outputs:
- loss: float32 [1], replicated
- image_grad: float32 [16384, 1152], P(('img', 'txt'))
- text_grad: float32 [16384, 1152], P(('txt', 'img'))
All inputs are finite; a program needn't handle non-finite values.
Results may differ from a plain program's by a relative error of at most 0.0016.
Values may be sent and summed in bfloat16 or wider, within the bound.
A program may use at most 64 MiB of HBM per device.

v0:
```python
import jax
import jax.numpy as jnp
from jax import lax
from jax.sharding import PartitionSpec as P


def unit_normalize(raw):
    values = raw.astype(jnp.float32)
    inverse = lax.rsqrt(jnp.sum(values * values, axis=1, keepdims=True) + 1e-06)
    return (values, inverse, (values * inverse).astype(jnp.bfloat16))


def restore(values, inverse, grads):
    inner = jnp.sum(values * grads, axis=1, keepdims=True)
    return inverse * grads - inverse * inverse * inverse * values * inner


def tile_terms(image_row_block, cols_y, row_base, target_start_index, inverse_warmth_factor, shift):
    dots = jnp.dot(image_row_block, cols_y.T, preferred_element_type=jnp.float32)
    logits = inverse_warmth_factor * dots + shift
    rows = row_base + jnp.arange(image_row_block.shape[0], dtype=jnp.int32)[:, None]
    cols = target_start_index + jnp.arange(cols_y.shape[0], dtype=jnp.int32)[None, :]
    positive = rows == cols
    label = jnp.where(positive, 1.0, -1.0).astype(jnp.float32)
    terms = jax.nn.softplus(-label * logits)
    weight = (jax.nn.sigmoid(logits) - positive.astype(jnp.float32)).astype(jnp.bfloat16)
    return (weight, jnp.sum(terms))


def local(picture_embeddings, caption_embeddings, sharpness_factor, pairing_shift):
    x_vals, x_inv, xn = unit_normalize(picture_embeddings)
    y_vals, y_inv, yn = unit_normalize(caption_embeddings)
    inverse_warmth_factor = sharpness_factor[0]
    shift = pairing_shift[0]
    x_block = lax.all_gather(xn, "txt", axis=0, tiled=True)
    y_block = lax.all_gather(yn, "img", axis=0, tiled=True)
    row_base = lax.axis_index("img") * x_block.shape[0]
    target_start_index = lax.axis_index("txt") * y_block.shape[0]
    weight, partial_loss_value = tile_terms(
        x_block, y_block, row_base, target_start_index, inverse_warmth_factor, shift
    )
    text_part = inverse_warmth_factor * lax.dot_general(
        weight, x_block, (((0,), (0,)), ((), ())), preferred_element_type=jnp.float32
    )
    image_part = inverse_warmth_factor * jnp.dot(
        weight, y_block, preferred_element_type=jnp.float32
    )
    gxn = lax.psum_scatter(image_part, "txt", scatter_dimension=0, tiled=True)
    gyn = lax.psum_scatter(text_part, "img", scatter_dimension=0, tiled=True)
    total = lax.psum(partial_loss_value, ("img", "txt"))
    pairs = x_block.shape[0] * lax.axis_size("img")
    loss = (total / pairs).reshape(1)
    return (loss, restore(x_vals, x_inv, gxn), restore(y_vals, y_inv, gyn))


def solution(mesh):
    in_specs = (P(("img", "txt"), None), P(("txt", "img"), None), P(), P())
    out_specs = (P(), P(("img", "txt"), None), P(("txt", "img"), None))
    return jax.shard_map(local, mesh=mesh, in_specs=in_specs, out_specs=out_specs, check_vma=False)
```

profile of v0, /device:TPU:1, one launch (start us, length us, event | category | flops | bytes accessed | tf_op | source)
XLA Modules:
  0.0 417.6 jit_solution(15902928895187648831)
XLA Ops:
  7.2 0.0 all-gather.5.cloned.1.call-start
  7.2 1.0 fusion.10
  8.3 1.7 fusion.11
  9.9 0.0 all-gather.5.cloned.1.call-update
  10.0 0.0 all-gather.3.cloned.1.call-start
  10.0 1.0 fusion.5
  11.1 1.7 fusion.6
  12.8 0.0 reduce-scatter.5.cloned.1.call-start
  14.1 26.7 %all-gather.5.cloned.1.call-done = bf16[512,1152]{1,0:T(8,128)(2,1)} async-done(((bf16[64,1152]{1,0:T(8,128)(2,1)}), bf16[512,1152]{1,0:T(8,128)(2,1)}) %all-gather.5.cloned.1.call-update) | async-done | bytes 1179664 | tf_op jit(solution)/shard_map/all_gather | solution.py:36
  40.9 83.6 %all-gather.3.cloned.1.call-done = bf16[2048,1152]{1,0:T(8,128)(2,1)} async-done(((bf16[64,1152]{1,0:T(8,128)(2,1)}), bf16[2048,1152]{1,0:T(8,128)(2,1)}) %all-gather.3.cloned.1.call-update) | async-done | bytes 4718608 | tf_op jit(solution)/shard_map/all_gather | solution.py:35
  124.4 8.9 %fusion.4 = (f32[]{:T(128)}, f32[2048,512]{1,0:T(8,128)S(1)}) fusion(f32[]{:T(128)} %bitcast.10, f32[]{:T(128)} %bitcast.7, s32[512]{0:T(512)S(1)} %iota_add_fusion.1, s32[2048]{0:T(1024)S(1)} %iota_add_fusion, bf16[2048,1152]{1,0:T(8,128)(2,1)} %all-gather.3.cloned.1.call-done, bf16[512,1152]{1,0:T(8,128)(2,1)} %all-gather.5.cloned.1.call-done), kind=kOutput, calls=%fused_computation.8 | convolution fusion | flops 2429550592 | bytes 10102796 | tf_op jit(solution)/shard_map/dot_general | solution.py:19
  133.3 2.1 copy-done.4
  135.4 4.7 %convolution_multiply_fusion.1 = f32[512,1152]{1,0:T(8,128)} fusion(bf16[2048,1152]{1,0:T(8,128)(2,1)S(1)} %copy-done.2, f32[]{:T(128)} %bitcast.9, f32[2048,512]{1,0:T(8,128)S(1)} %get-tuple-element.8, f32[]{:T(128)} %bitcast.12, s32[512]{0:T(512)S(1)} %iota_add_fusion.1, s32[2048]{0:T(1024)S(1)} %iota_add_fusion), kind=kOutput, calls=%fused_computation.10 | convolution fusion | flops 2425946112 | bytes 11282440 | tf_op jit(solution)/shard_map/dot_general | solution.py:42
  140.1 0.0 reduce-scatter.5.cloned.1.call-update
  140.1 0.0 reduce-scatter.3.cloned.1.call-start
  140.1 9.6 %convolution_multiply_fusion = f32[2048,1152]{1,0:T(8,128)} fusion(bf16[512,1152]{1,0:T(8,128)(2,1)S(1)} %copy-done.3, f32[]{:T(128)} %bitcast.8, f32[2048,512]{1,0:T(8,128)} %copy-done.4, f32[]{:T(128)} %bitcast.11, s32[512]{0:T(512)S(1)} %iota_add_fusion.1, s32[2048]{0:T(1024)S(1)} %iota_add_fusion), kind=kOutput, calls=%fused_computation.1 | convolution fusion | flops 2427715584 | bytes 14821384 | tf_op jit(solution)/shard_map/dot_general | solution.py:45
  149.8 0.0 reduce-scatter.3.cloned.1.call-update
  149.8 78.3 %psum.7 = f32[]{:T(128)} all-reduce(f32[]{:T(128)} %get-tuple-element.7), channel_id=1, replica_groups=mesh['img'=8,'txt'=32] {'img','txt'}, use_global_device_ids=true, to_apply=%region_3.4 | all-reduce | flops 1 | bytes 8 | tf_op jit(solution)/shard_map/psum | solution.py:50
  228.8 0.0 reduce-scatter.5.cloned.1.call-done
  228.8 1.1 fusion.14
  229.9 1.8 fusion.13
  231.7 175.3 %reduce-scatter.3.cloned.1.call-done = f32[64,1152]{1,0:T(8,128)} async-done(((f32[2048,1152]{1,0:T(8,128)}), f32[64,1152]{1,0:T(8,128)}) %reduce-scatter.3.cloned.1.call-update) | async-done | bytes 294928 | tf_op jit(solution)/shard_map/reduce_scatter | solution.py:48
  407.0 1.1 fusion.9
  408.1 1.8 fusion.8
  (14 shorter events, 0.1 us)
Async XLA Ops:
  7.2 33.7 %all-gather.5.cloned.1.call-start = ((), (), s32[]{:S(2)}) async-start(), calls=%async_computation.3 | async-start | bytes 1327104 | tf_op jit(solution)/shard_map/all_gather | solution.py:36
  10.0 114.5 %all-gather.3.cloned.1.call-start = ((), (), s32[]{:S(2)}) async-start(), calls=%async_computation.2 | async-start | bytes 4866048 | tf_op jit(solution)/shard_map/all_gather | solution.py:35
  12.8 216.0 %reduce-scatter.5.cloned.1.call-start = ((), (), s32[]{:S(2)}) async-start(), calls=%async_computation.5 | async-start | bytes 2654208 | tf_op jit(solution)/shard_map/reduce_scatter | solution.py:49
  124.4 10.9 %copy-start.2 = (bf16[2048,1152]{1,0:T(8,128)(2,1)S(1)}, bf16[2048,1152]{1,0:T(8,128)(2,1)}, u32[]{:S(2)}) copy-start(bf16[2048,1152]{1,0:T(8,128)(2,1)} %all-gather.3.cloned.1.call-done) | copy-start | bytes 14155780
  133.3 2.1 copy-start.4
  135.4 4.8 %copy-start.3 = (bf16[512,1152]{1,0:T(8,128)(2,1)S(1)}, bf16[512,1152]{1,0:T(8,128)(2,1)}, u32[]{:S(2)}) copy-start(bf16[512,1152]{1,0:T(8,128)(2,1)} %all-gather.5.cloned.1.call-done) | copy-start | bytes 3538948
  140.1 267.0 %reduce-scatter.3.cloned.1.call-start = ((), (), s32[]{:S(2)}) async-start(), calls=%async_computation.4 | async-start | bytes 9732096 | tf_op jit(solution)/shard_map/reduce_scatter | solution.py:48
  149.8 79.0 %copy-start = (bf16[64,1152]{1,0:T(8,128)(2,1)S(1)}, bf16[64,1152]{1,0:T(8,128)(2,1)}, u32[]{:S(2)}) copy-start(bf16[64,1152]{1,0:T(8,128)(2,1)} %param.5) | copy-start | bytes 442372
  149.8 257.3 %copy-start.1 = (bf16[64,1152]{1,0:T(8,128)(2,1)S(1)}, bf16[64,1152]{1,0:T(8,128)(2,1)}, u32[]{:S(2)}) copy-start(bf16[64,1152]{1,0:T(8,128)(2,1)} %param.4) | copy-start | bytes 442372
Sparse Core Ops, SparseCore 0:
  10.4 30.4 all-gather.4
  44.0 80.3 all-gather.2
  140.2 34.5 reduce-scatter.4
  178.7 228.3 reduce-scatter.2
where the time goes:
time: 421 us; the launch traced here: 418 us
  waiting for transfers between devices  286 us (68%)
  blocking collectives  78.3 us (19%)
  matrix products  23.2 us (6%)
  between operations  16.9 us (4%)
  other arithmetic  11.2 us (3%)
    reduce_scatter x1, waiting for transfers between devices, local(): gxn = lax.psum_scatter(image_part, 'txt', scatter_dimension=0, tiled=True)  175 us
    all_gather x1, waiting for transfers between devices, local(): x_block = lax.all_gather(xn, 'txt', axis=0, tiled=True)  83.6 us
    psum x1, blocking collectives, local(): total = lax.psum(partial_loss_value, ('img', 'txt'))  78.3 us
    all_gather x1, waiting for transfers between devices, local(): y_block = lax.all_gather(yn, 'img', axis=0, tiled=True)  26.7 us
    dot_general x1, matrix products, local(): jnp.dot(weight, y_block, preferred_element_type=jnp.float32)  9.63 us
    dot_general x1, matrix products, tile_terms(): jnp.dot(image_row_block, cols_y.T, preferred_element_type=jnp.float32)  8.86 us
  transfers between devices with their start and end apart: 4, of which 3 were waited for; matrix products, arithmetic and copies ran while one was open for 4% of the time, Pallas kernels for 0%

commit v1 on v0

v1 whole, which is shorter than its diff:
```python
import jax
import jax.numpy as jnp
from jax import lax
from jax.experimental import pallas as pl
from jax.experimental.pallas import tpu as pltpu
from jax.sharding import PartitionSpec as P

MESH = pl.DeviceIdType.MESH
F32 = jnp.float32
BF16 = jnp.bfloat16
ROWS = 64
HALF = 32
D = 1152
POS = {0: 0, 4: 1, 1: 2, 7: 3, 2: 4, 6: 5, 3: 6, 5: 7}


def encode(v):
    return (v * jnp.abs(v)).astype(BF16)


def decode(u):
    u = u.astype(F32)
    return u * lax.rsqrt(jnp.maximum(jnp.abs(u), 1e-37))


def kernel(x_ref, y_ref, scale_ref, shift_ref, loss_ref, gx_ref, gy_ref,
           xg, yg, w, own, isend, irecv, p2, p2send, p2recv, tf, crecv, zsend, zrecv,
           lacc, lsum, lrecv, ssem, rsem):
    img, txt = lax.axis_index("img"), lax.axis_index("txt")
    Y, C = img // 2, img % 2
    X, Z = txt // 8, txt % 8

    def dev(dx=0, dy=0, dz=0, dc=0):
        return (((Y + dy) % 4) * 2 + (C + dc) % 2, ((X + dx) % 4) * 8 + (Z + dz) % 8)

    count = [0]

    def copy(src, dst, to):
        i = count[0]
        count[0] += 1
        c = pltpu.make_async_remote_copy(src_ref=src, dst_ref=dst, send_sem=ssem.at[i], recv_sem=rsem.at[i],
                                         device_id=to, device_id_type=MESH)
        started.append(c)
        return c

    started = []
    barrier = pltpu.get_barrier_semaphore()
    peers = ([dev(dx=i) for i in (1, 2, 3)] + [dev(dy=i) for i in (1, 2, 3)]
             + [dev(dz=i) for i in range(1, 8)] + [dev(dc=1)])
    for p in peers:
        pl.semaphore_signal(barrier, inc=1, device_id=p, device_id_type=MESH)

    def unit(ref):
        values = ref[...].astype(F32)
        inverse = lax.rsqrt(jnp.sum(values * values, axis=1, keepdims=True) + 1e-06)
        return (values * inverse).astype(BF16)

    def A(k, j):
        return k * 256 + j * HALF

    def B(k, j):
        return k * 256 + 128 + j * HALF

    def yrow(s, rc):
        return POS[s] * 128 + rc * ROWS

    yn = unit(y_ref)
    yg[pl.ds(yrow(0, 0), ROWS)] = yn
    xn = unit(x_ref)
    xg[pl.ds(A(0, 0), HALF)] = xn[:HALF]
    xg[pl.ds(B(0, 0), HALF)] = xn[HALF:]
    pl.semaphore_wait(barrier, len(peers))

    def ydma(s_from, s_to, h, dz):
        return copy(yg.at[pl.ds(yrow(s_from, 0) + h * HALF, HALF)], yg.at[pl.ds(yrow(s_to, 0) + h * HALF, HALF)], dev(dz=dz))

    def xdma(a, b, n, to):
        return copy(xg.at[pl.ds(a, n)], xg.at[pl.ds(b, n)], to)

    def ycore(s):
        c = copy(yg.at[pl.ds(yrow(s, 0), ROWS)], yg.at[pl.ds(yrow(s, 1), ROWS)], dev(dc=1))
        c.start()
        return c

    up, down, cores = {}, {}, {}
    for h in (0, 1):
        up[1, h] = ydma(0, 7, h, 1)
        down[1, h] = ydma(0, 1, h, -1)
        up[1, h].start()
        down[1, h].start()
    fa, fb = {}, {}
    for j, d in ((3, 1), (1, -1), (2, 2)):
        fa[j] = xdma(A(0, 0), A(0, j), HALF, dev(dx=d))
        fb[j] = xdma(B(0, 0), B(0, j), HALF, dev(dy=d))
        fa[j].start()
        fb[j].start()
    sa, sb = {}, {}

    def second(j):
        for k, d in ((3, 1), (1, -1)):
            sa[k, j] = xdma(A(0, j), A(k, j), HALF, dev(dy=d))
            sb[k, j] = xdma(B(0, j), B(k, j), HALF, dev(dx=d))
            sa[k, j].start()
            sb[k, j].start()

    ta, tb = {}, {}

    def third(j):
        for k, d, o in ((3, 1, 16), (1, -1, 0)):
            sa[k, j].wait_recv()
            ta[k, j] = xdma(A(k, j) + o, A(2, j) + o, 16, dev(dy=d))
            ta[k, j].start()
            sb[k, j].wait_recv()
            tb[k, j] = xdma(B(k, j) + o, B(2, j) + o, 16, dev(dx=d))
            tb[k, j].start()

    def ystep(t):
        for h in (0, 1):
            if t <= 4:
                up[t - 1, h].wait_recv()
                if t < 4 or h == 0:
                    up[t, h] = ydma((9 - t) % 8, 8 - t, h, 1)
                    up[t, h].start()
                down[t - 1, h].wait_recv()
                if t < 4 or h == 1:
                    down[t, h] = ydma(t - 1, t, h, -1)
                    down[t, h].start()
        if t == 5:
            up[4, 0].wait_recv()
            down[4, 1].wait_recv()
            cores[4] = ycore(4)
        else:
            cores[9 - t] = ycore(9 - t)
            cores[t - 1] = ycore(t - 1)

    second(0)
    cores[0] = ycore(0)
    for j in (1, 3):
        fa[j].wait_recv()
        fb[j].wait_recv()
        second(j)
    ystep(2)
    fa[2].wait_recv()
    fb[2].wait_recv()
    second(2)
    third(0)
    ystep(3)
    third(1)
    ystep(4)
    third(3)
    ystep(5)
    third(2)
    for j in range(4):
        for k in (1, 3):
            ta[k, j].wait_recv()
            tb[k, j].wait_recv()
    for s in range(8):
        cores[s].wait_recv()

    scale = scale_ref[0]
    shift = shift_ref[0]
    lacc[...] = jnp.zeros_like(lacc)

    def tile(i, _):
        k = pl.multiple_of((i // 4) * 256, 256)
        g = pl.multiple_of((i % 4) * 256, 256)
        dots = lax.dot_general(xg[pl.ds(k, 256), :], yg[pl.ds(g, 256), :], (((1,), (1,)), ((), ())),
                               preferred_element_type=F32)
        e = jnp.exp(scale * dots + shift)
        d = 1.0 + e
        w[pl.ds(k, 256), pl.ds(g, 256)] = (e / d).astype(BF16)
        lacc[...] += jnp.sum(jnp.log1p(e).reshape(32, 8, 256), axis=0)
        return 0

    lax.fori_loop(0, 16, tile, 0)

    @pl.when(Y == Z // 2)
    def _():
        rc = (Z + C) % 2
        for xx in range(4):
            for h in (0, 1):
                k, j = (X - Y + 4) % 4, (xx - X + 4) % 4
                row = k * 256 + j * HALF if h == 0 else j * 256 + 128 + k * HALF
                row = pl.multiple_of(row, HALF)
                s = (4 * C + xx - Z + 8) % 8
                pos = jnp.where(s == 0, 0, jnp.where(s == 4, 1, jnp.where(s < 4, 2 * s, 2 * (8 - s) + 1)))
                col = pl.multiple_of(pos * 128, 128)
                yr = pl.multiple_of(pos * 128 + rc * ROWS + h * HALF, HALF)
                xv = xg[pl.ds(row, HALF), :].astype(F32)
                yv = yg[pl.ds(yr, HALF), :].astype(F32)
                z = scale * jnp.sum(xv * yv, axis=1, keepdims=True) + shift
                e = jnp.exp(z)
                wd = (e / (1.0 + e) - 1.0).astype(BF16)
                lane = lax.broadcasted_iota(jnp.int32, (HALF, 128), 1)
                sub = lax.broadcasted_iota(jnp.int32, (HALF, 128), 0)
                hit = lane == sub + rc * ROWS + h * HALF
                old = w[pl.ds(row, HALF), pl.ds(col, 128)]
                w[pl.ds(row, HALF), pl.ds(col, 128)] = jnp.where(hit, wd.astype(F32), old.astype(F32)).astype(BF16)
                zz = jnp.where(hit, z, 0.0)
                lacc[:, :128] -= jnp.sum(zz.reshape(4, 8, 128), axis=0)

    lcopies = {}

    def lsend(axis):
        n, me, base, kw = {"c": (2, C, 0, "dc"), "z": (8, Z, 2, "dz"), "x": (4, X, 10, "dx"), "y": (4, Y, 14, "dy")}[axis]
        v = jnp.sum(lacc[...]) if axis == "c" else lsum[0, 0]
        lrecv[base + me] = jnp.full((8, 128), v, F32)
        for o in range(1, n):
            c = copy(lrecv.at[base + me], lrecv.at[base + me], dev(**{kw: o}))
            c.start()
            lcopies[axis, o] = c

    def lwait(axis):
        n, base = {"c": (2, 0), "z": (8, 2), "x": (4, 10), "y": (4, 14)}[axis]
        for o in range(1, n):
            lcopies[axis, o].wait_recv()
        t = lrecv[base]
        for o in range(1, n):
            t = t + lrecv[base + o]
        lsum[...] = t

    lsend("c")

    cr = {}

    def text(g):
        tf[pl.ds(g * 256, 256), :] = lax.dot_general(w[:, pl.ds(g * 256, 256)], xg[...], (((0,), (0,)), ((), ())),
                                                     preferred_element_type=F32)
        for s in range(8):
            if POS[s] // 2 == g:
                cr[s] = copy(tf.at[pl.ds(yrow(s, 1), ROWS)], crecv.at[pl.ds(s * ROWS, ROWS)], dev(dc=1))
                cr[s].start()

    pa, pb = {}, {}

    def image(k):
        part = jnp.dot(w[pl.ds(k * 256, 256), :], yg[...], preferred_element_type=F32)
        if k == 0:
            own[...] = part
            return
        o = (k - 1) * 256
        isend[pl.ds(o, 256), :] = encode(part)
        pa[k] = copy(isend.at[pl.ds(o, 128)], irecv.at[pl.ds(o, 128)], dev(dy=k))
        pb[k] = copy(isend.at[pl.ds(o + 128, 128)], irecv.at[pl.ds(o + 128, 128)], dev(dx=k))
        pa[k].start()
        pb[k].start()

    def add_core(s):
        cr[s].wait_recv()
        tf[pl.ds(yrow(s, 0), ROWS), :] += crecv[pl.ds(s * ROWS, ROWS), :]

    zc = {}
    zslots = {}

    def zhop(direction, t, h):
        s = t if direction > 0 else 8 - t
        v = tf[pl.ds(yrow(s, 0) + h * HALF, HALF), :]
        first = 4 if (direction > 0) == (h == 0) else 3
        if t < first:
            zc[direction, t + 1, h].wait_recv()
            r = zslots[direction, t + 1, h]
            v = v + decode(zrecv[pl.ds(r, HALF), :])
        r = len(zslots) * HALF
        zslots[direction, t, h] = r
        zsend[pl.ds(r, HALF), :] = encode(v)
        zc[direction, t, h] = copy(zsend.at[pl.ds(r, HALF)], zrecv.at[pl.ds(r, HALF)], dev(dz=direction))
        zc[direction, t, h].start()

    text(0)
    image(2)
    add_core(4)
    add_core(0)
    zhop(1, 4, 0)
    zhop(-1, 4, 1)
    text(3)
    lwait("c")
    lsend("z")
    add_core(3)
    add_core(5)
    zhop(1, 3, 1)
    zhop(-1, 3, 0)
    image(1)
    image(3)
    zhop(1, 3, 0)
    zhop(-1, 3, 1)
    lwait("z")
    lsend("x")
    text(2)
    add_core(2)
    add_core(6)
    zhop(1, 2, 1)
    zhop(-1, 2, 0)
    zhop(1, 2, 0)
    zhop(-1, 2, 1)
    text(1)
    add_core(1)
    add_core(7)
    zhop(1, 1, 1)
    zhop(-1, 1, 0)
    image(0)
    lwait("x")
    lsend("y")

    for k in (1, 3, 2):
        pa[k].wait_recv()
        pb[k].wait_recv()
        own[...] += decode(irecv[pl.ds((k - 1) * 256, 256), :])
    qa, qb = {}, {}
    for n, j in enumerate((2, 1, 3)):
        p2send[pl.ds(n * 64, HALF), :] = encode(own[pl.ds(j * HALF, HALF), :])
        p2send[pl.ds(n * 64 + HALF, HALF), :] = encode(own[pl.ds(128 + j * HALF, HALF), :])
        qa[j] = copy(p2send.at[pl.ds(n * 64, HALF)], p2recv.at[pl.ds(n * 64, HALF)], dev(dx=j))
        qb[j] = copy(p2send.at[pl.ds(n * 64 + HALF, HALF)], p2recv.at[pl.ds(n * 64 + HALF, HALF)], dev(dy=j))
        qa[j].start()
        qb[j].start()
    zhop(1, 1, 0)
    zhop(-1, 1, 1)

    def restore(ref, grads):
        values = ref[...].astype(F32)
        inverse = lax.rsqrt(jnp.sum(values * values, axis=1, keepdims=True) + 1e-06)
        inner = jnp.sum(values * grads, axis=1, keepdims=True)
        return inverse * grads - inverse * inverse * inverse * values * inner

    p2[pl.ds(0, HALF), :] = own[pl.ds(0, HALF), :]
    p2[pl.ds(HALF, HALF), :] = own[pl.ds(128, HALF), :]
    for n, j in enumerate((2, 1, 3)):
        qa[j].wait_recv()
        qb[j].wait_recv()
        p2[...] += decode(p2recv[pl.ds(n * 64, 64), :])
    gx_ref[...] = restore(x_ref, scale * p2[...])

    lwait("y")
    loss_ref[0] = lsum[0, 0] / 16384.0

    for h in (0, 1):
        for direction in (1, -1):
            zc[direction, 1, h].wait_recv()
            r = zslots[direction, 1, h]
            tf[pl.ds(h * HALF, HALF), :] += decode(zrecv[pl.ds(r, HALF), :])
    gy_ref[...] = restore(y_ref, scale * tf[pl.ds(0, ROWS), :])
    for c in started:
        c.wait_send()


COPIES = 120


def local(picture_embeddings, caption_embeddings, sharpness_factor, pairing_shift):
    vmem = pl.BlockSpec(memory_space=pltpu.VMEM)
    smem = pl.BlockSpec(memory_space=pltpu.SMEM)
    return pl.pallas_call(
        kernel,
        out_shape=(
            jax.ShapeDtypeStruct((1,), F32),
            jax.ShapeDtypeStruct((ROWS, D), F32),
            jax.ShapeDtypeStruct((ROWS, D), F32),
        ),
        in_specs=[vmem, vmem, smem, smem],
        out_specs=(smem, vmem, vmem),
        scratch_shapes=[
            pltpu.VMEM((1024, D), BF16),
            pltpu.VMEM((1024, D), BF16),
            pltpu.VMEM((1024, 1024), BF16),
            pltpu.VMEM((256, D), F32),
            pltpu.VMEM((768, D), BF16),
            pltpu.VMEM((768, D), BF16),
            pltpu.VMEM((ROWS, D), F32),
            pltpu.VMEM((192, D), BF16),
            pltpu.VMEM((192, D), BF16),
            pltpu.VMEM((1024, D), F32),
            pltpu.VMEM((512, D), F32),
            pltpu.VMEM((14 * HALF, D), BF16),
            pltpu.VMEM((14 * HALF, D), BF16),
            pltpu.VMEM((8, 256), F32),
            pltpu.VMEM((8, 128), F32),
            pltpu.VMEM((18, 8, 128), F32),
            pltpu.SemaphoreType.DMA((COPIES,)),
            pltpu.SemaphoreType.DMA((COPIES,)),
        ],
        compiler_params=pltpu.CompilerParams(collective_id=0, has_side_effects=True, vmem_limit_bytes=56 * 2**20),
    )(picture_embeddings, caption_embeddings, sharpness_factor, pairing_shift)


def solution(mesh):
    in_specs = (P(("img", "txt"), None), P(("txt", "img"), None), P(), P())
    out_specs = (P(), P(("img", "txt"), None), P(("txt", "img"), None))
    return jax.shard_map(local, mesh=mesh, in_specs=in_specs, out_specs=out_specs, check_vma=False)
```

time: 421 us -> 72.2 us (0.17)
  waiting for transfers between devices: 286 us -> 0 us
  blocking collectives: 78.3 us -> 0 us
  Pallas kernels: 0 us -> 65.5 us
  matrix products: 23.2 us -> 0 us
  between operations: 16.9 us -> 3.74 us
  other arithmetic: 11.2 us -> 0 us
    reduce_scatter x2 -> x0, waiting for transfers between devices: 175 us -> none  [the longest x1 175 us: local(): gxn = lax.psum_scatter(image_part, 'txt', scatter_dimension=0, tiled=True)]
    all_gather x2 -> x0, waiting for transfers between devices: 110 us -> none  [the longest x1 83.6 us: local(): x_block = lax.all_gather(xn, 'txt', axis=0, tiled=True)]
    psum x1 -> x0, blocking collectives: 78.3 us -> none  [local(): total = lax.psum(partial_loss_value, ('img', 'txt'))]
    pallas_call x0 -> x1, Pallas kernels: none -> 65.5 us  [local(): pl.pallas_call(kernel, out_shape=(jax.ShapeDtypeStruct((1,), F32), jax.Sh...]
    dot_general x3 -> x0, matrix products: 23.2 us -> none  [the longest x1 9.63 us: local(): jnp.dot(weight, y_block, preferred_element_type=jnp.float32)]
    reduce_sum x4 -> x0, other arithmetic: 4.27 us -> none  [the longest x2 2.19 us: restore(): inner = jnp.sum(values * grads, axis=1, keepdims=True)]
  transfers between devices with their start and end apart: 4 -> 0, of which waited for: 3 -> 0; matrix products, arithmetic and copies ran while one was open for 4% -> 0% of each run, Pallas kernels for 0% -> 0%
where the time goes in v1:
time: 72.2 us; the launch traced here: 71.7 us
  Pallas kernels  65.5 us (91%)
  between operations  3.74 us (5%)
  local copies, waits for them, and re-layouts  2.46 us (3%)
    pallas_call x1, Pallas kernels, local(): pl.pallas_call(kernel, out_shape=(jax.ShapeDtypeStruct((1,), F32), jax.Sh...  65.5 us
    unnamed x4, local copies, waits for them, and re-layouts  2.46 us

profile of v1, /device:TPU:1, one launch (start us, length us, event | category | flops | bytes accessed | tf_op | source)
XLA Modules:
  0.0 71.7 jit_solution(3985396204305382111)
XLA Ops:
  1.9 65.5 %shard_map.67 = (f32[1]{0:T(128)}, f32[64,1152]{1,0:T(8,128)}, f32[64,1152]{1,0:T(8,128)}) custom-call(bf16[64,1152]{1,0:T(8,128)(2,1)} %x_ref.1, bf16[64,1152]{1,0:T(8,128)(2,1)} %y_ref.1, f32[1]{0:T(128)S(6)} %copy.10.scale_ref, f32[1]{0:T(128)S(6)} %copy.11.shift_ref), custom_call_target="tpu_custom_call" | custom-call | tf_op jit(solution)/shard_map/pallas_call | solution.py:352
  68.1 0.0 copy-start
  68.2 1.7 %copy.13 = f32[64,1152]{1,0:T(8,128)} copy(f32[64,1152]{1,0:T(8,128)} %get-tuple-element.7) | data formatting | bytes 589824
  69.9 0.0 copy-done
  69.9 0.7 copy.14
Async XLA Ops:
  68.1 1.8 %copy-start = (f32[64,1152]{1,0:T(8,128)S(1)}, f32[64,1152]{1,0:T(8,128)}, u32[]{:S(2)}) copy-start(f32[64,1152]{1,0:T(8,128)} %get-tuple-element.8) | copy-start | bytes 884740

commit v2 on v0

v2 whole, which is shorter than its diff:
```python
import jax
import jax.numpy as jnp
from jax import lax
from jax.experimental import pallas as pl
from jax.experimental.pallas import tpu as pltpu
from jax.sharding import PartitionSpec as P

MESH = pl.DeviceIdType.MESH
F32 = jnp.float32
BF16 = jnp.bfloat16
ROWS = 64
HALF = 32
PIECE = 16
D = 1152
LOG2E = 1.4426950408889634
POS = {0: 0, 1: 1, 7: 2, 2: 3, 6: 4, 3: 5, 5: 6, 4: 7}
CHUNK = {0: 0, 1: 1, 3: 2, 2: 3}
RATE = {"core": 300.0}
LINK_RATE = 20.6
LATENCY = {"core": 0.8, 1: 2.0, 2: 2.7}
BACKLOG = 1.6
ISSUE = 0.03
WAIT = 0.015


class Schedule:
    def __init__(self):
        self.tasks = {}

    def op(self, name, cost, deps, fn):
        self.tasks[name] = dict(name=name, msg=False, cost=cost, deps=list(deps), fn=fn)

    def msg(self, name, links, rows, lat, deps, make, sent, come):
        took = max([rows / RATE.get(x, LINK_RATE) for x in links], default=0.0)
        self.tasks[name] = dict(name=name, msg=True, links=links, took=took, lat=lat, deps=list(deps), fn=make, sent=sent, come=come)

    def levels(self):
        users = {n: [] for n in self.tasks}
        for n, t in self.tasks.items():
            for d in t["deps"]:
                users[d].append(n)
        level = {}

        def visit(n):
            if n not in level:
                t = self.tasks[n]
                own = ISSUE + t["lat"] + t["took"] if t["msg"] else t["cost"]
                level[n] = own + max([visit(u) for u in users[n]], default=0.0)
            return level[n]

        for n in self.tasks:
            visit(n)
        return level

    def order(self):
        level = self.levels()
        now, arrived, free, out, waited = 0.0, {}, {}, [], set()
        left = list(self.tasks)
        self.times = {}
        while left:
            ready, later = [], []
            for n in left:
                t = self.tasks[n]
                if any(d not in arrived for d in t["deps"]):
                    continue
                at = max([arrived[d] for d in t["deps"]] + [free.get(x, 0.0) - BACKLOG for x in t.get("links", ())], default=0.0)
                if at <= now + 1e-9:
                    ready.append(n)
                else:
                    later.append(at)
            if not ready:
                now = min(later)
                continue
            n = max(ready, key=lambda n: (self.tasks[n]["msg"], level[n]))
            left.remove(n)
            out.append(n)
            t = self.tasks[n]
            for d in t["deps"]:
                if self.tasks[d]["msg"] and d not in waited:
                    waited.add(d)
                    now += WAIT
            if t["msg"]:
                now += ISSUE
                end = max([now] + [free.get(x, 0.0) for x in t["links"]]) + t["took"]
                for x in t["links"]:
                    free[x] = end
                arrived[n] = end + t["lat"]
            else:
                now += t["cost"]
                arrived[n] = now
            self.times[n] = now
        return out

    def emit(self, ssem, rsem, sizes):
        number = {True: {}, False: {}}
        members = {}
        for n, t in self.tasks.items():
            if t["msg"]:
                number[True].setdefault(t["sent"], len(number[True]))
                number[False].setdefault(t["come"], len(number[False]))
                members.setdefault(t["come"], []).append(n)
        assert len(number[True]) <= SENT and len(number[False]) <= COME, "semaphores"
        copies, received = {}, set()

        def wait_group(sem, ref):
            pltpu.make_async_copy(ref, ref, sem).wait()

        def receive(come):
            if come in received:
                return
            received.add(come)
            assert all(m in copies for m in members[come]), "group"
            if len(members[come]) == 1:
                copies[members[come][0]].wait_recv()
            else:
                wait_group(rsem.at[number[False][come]], sizes[come])

        for n in self.order():
            t = self.tasks[n]
            for d in t["deps"]:
                if self.tasks[d]["msg"]:
                    receive(self.tasks[d]["come"])
            if t["msg"]:
                copies[n] = t["fn"](ssem.at[number[True][t["sent"]]], rsem.at[number[False][t["come"]]])
                copies[n].start()
            else:
                t["fn"]()
        for come in members:
            receive(come)
        for sent, i in number[True].items():
            wait_group(ssem.at[i], sizes[sent])


def encode(v):
    return (v * jnp.abs(v)).astype(BF16)


def decode(u):
    u = u.astype(F32)
    return u * lax.rsqrt(jnp.maximum(jnp.abs(u), 1e-37))


def log1p(p):
    small = p * (1.0 - p * (0.5 - p * (1.0 / 3.0 - p * 0.25)))
    return jnp.where(p < 0.01, small, jnp.log(1.0 + p))


def kernel(x_ref, y_ref, scale_ref, shift_ref, out_ref,
           xg, yg, w, imf, isend, irecv, p2send, p2recv, tf, crecv, zsend, zrecv,
           lacc, lsum, lrecv, ssem, rsem):
    img, txt = lax.axis_index("img"), lax.axis_index("txt")
    Y, C = img // 2, img % 2
    X, Z = txt // 8, txt % 8

    def dev(dx=0, dy=0, dz=0, dc=0):
        return (((Y + dy) % 4) * 2 + (C + dc) % 2, ((X + dx) % 4) * 8 + (Z + dz) % 8)

    barrier = pltpu.get_barrier_semaphore()
    peers = ([dev(dz=i) for i in range(1, 8)] + [dev(dx=i) for i in (1, 2, 3)] + [dev(dy=i) for i in (1, 2, 3)]
             + [dev(dc=1)])
    for p in peers:
        pl.semaphore_signal(barrier, inc=1, device_id=p, device_id_type=MESH)

    def unit(ref):
        values = ref[...].astype(F32)
        inverse = lax.rsqrt(jnp.sum(values * values, axis=1, keepdims=True) + 1e-06)
        return (values * inverse).astype(BF16)

    def A(k, j):
        return CHUNK[k] * 256 + j * HALF

    def B(k, j):
        return CHUNK[k] * 256 + 128 + j * HALF

    def yrow(s, rc):
        return POS[s] * 128 + rc * ROWS

    scale = scale_ref[0]
    shift = shift_ref[0]

    g = Schedule()

    def send(name, links, rows, deps, src, dst, to, sent, come=None, lat=None):
        if lat is None:
            lat = LATENCY["core"] if links == ["core"] else LATENCY[len(links)]
        g.msg(name, links, rows, lat, deps, lambda ss, rs: pltpu.make_async_remote_copy(
            src_ref=src, dst_ref=dst, send_sem=ss, recv_sem=rs, device_id=to, device_id_type=MESH), sent, come or name)

    def own_text():
        yg[pl.ds(yrow(0, 0), ROWS)] = unit(y_ref)
        pl.semaphore_wait(barrier, len(peers))

    def own_image():
        xn = unit(x_ref)
        xg[pl.ds(A(0, 0), HALF)] = xn[:HALF]
        xg[pl.ds(B(0, 0), HALF)] = xn[HALF:]
        lacc[...] = jnp.zeros_like(lacc)

    g.op("ny", 0.3, [], own_text)
    g.op("nx", 0.3, ["ny"], own_image)

    def rows_of(ref, start, n):
        return ref.at[pl.ds(start, n)]

    for t in (1, 2, 3, 4):
        for h in range(ROWS // PIECE):
            o = h * PIECE
            if t < 4 or o < HALF:
                send(f"u{t}{h}", ["z+"], PIECE, [f"u{t - 1}{h}"] if t > 1 else ["ny"],
                     rows_of(yg, yrow((9 - t) % 8, 0) + o, PIECE), rows_of(yg, yrow(8 - t, 0) + o, PIECE), dev(dz=1), "SY", "R4" if t == 4 else None)
            if t < 4 or o >= HALF:
                send(f"d{t}{h}", ["z-"], PIECE, [f"d{t - 1}{h}"] if t > 1 else ["ny"],
                     rows_of(yg, yrow(t - 1, 0) + o, PIECE), rows_of(yg, yrow(t, 0) + o, PIECE), dev(dz=-1), "SY", "R4" if t == 4 else None)
    pieces = range(ROWS // PIECE)
    yhave = {0: ["ny"], 4: [f"u4{h}" for h in pieces if h * PIECE < HALF] + [f"d4{h}" for h in pieces if h * PIECE >= HALF]}
    for t in (1, 2, 3):
        yhave[8 - t] = [f"u{t}{h}" for h in pieces]
        yhave[t] = [f"d{t}{h}" for h in pieces]
    for s in range(8):
        send(f"c{s}", ["core"], ROWS, yhave[s], rows_of(yg, yrow(s, 0), ROWS), rows_of(yg, yrow(s, 1), ROWS), dev(dc=1), "SC")

    def both(name, d, rows, da, db, a, a2, b, b2, n):
        links = {1: ["{}+"], 3: ["{}-"], 2: ["{}+", "{}-"]}[d % 4]
        first = name[0] == "f"
        come = "RT" if name[0] == "t" else "R" + name
        ax, bx = ("x", "y") if first else ("y", "x")
        send(name + "a", [x.format(ax) for x in links], rows, da, rows_of(xg, a, n), rows_of(xg, a2, n), dev(**{"d" + ax: d}), "SX", come)
        send(name + "b", [x.format(bx) for x in links], rows, db, rows_of(xg, b, n), rows_of(xg, b2, n), dev(**{"d" + bx: d}), "SX", come)

    for j, d in ((3, 1), (1, -1), (2, 2)):
        both(f"f{j}", d, HALF, ["nx"], ["nx"], A(0, 0), A(0, j), B(0, 0), B(0, j), HALF)
    for j in range(4):
        for k, d in ((3, 1), (1, -1)):
            da = db = [f"f{j}a", f"f{j}b"] if j else ["nx"]
            both(f"s{k}{j}", d, HALF, da, db, A(0, j), A(k, j), B(0, j), B(k, j), HALF)
            o = 16 if k == 3 else 0
            both(f"t{k}{j}", d, 16, [f"s{k}{j}a", f"s{k}{j}b"], [f"s{k}{j}a", f"s{k}{j}b"], A(k, j) + o, A(2, j) + o, B(k, j) + o, B(2, j) + o, 16)
    xhave = {0: [f"f{j}{q}" for j in (1, 2, 3) for q in "ab"], 2: [f"t{k}{j}{q}" for k in (1, 3) for j in range(4) for q in "ab"]}
    for k in (1, 3):
        xhave[k] = [f"s{k}{j}{q}" for j in range(4) for q in "ab"]

    def tile(r0, nr, c0, nc):
        def run():
            dots = lax.dot_general(xg[pl.ds(r0, nr), :], yg[pl.ds(c0, nc), :], (((1,), (1,)), ((), ())),
                                   preferred_element_type=F32)
            e = jnp.exp2(dots * (scale * LOG2E) + shift * LOG2E)
            d = 1.0 + e
            r = pl.reciprocal(d, approx=True)
            r = r * (2.0 - d * r)
            w[pl.ds(r0, nr), pl.ds(c0, nc)] = (e * r).astype(BF16)
            m = nr // 8
            n = m // 3
            e, d = e.reshape(m, 8, nc), d.reshape(m, 8, nc)
            p = e[:n] * d[n : 2 * n] + e[n : 2 * n]
            p = p * d[2 * n : 3 * n] + e[2 * n : 3 * n]
            total = jnp.sum(log1p(p), axis=0)
            if m - 3 * n == 2:
                total += log1p(e[m - 2] * d[m - 1] + e[m - 1])
            elif m - 3 * n == 1:
                total += log1p(e[m - 1])
            for c in range(0, nc, 128):
                lacc[...] += total[:, c : c + 128]

        return run

    groups = {"a": (0, 384, (0, 1, 7)), "b": (384, 256, (2, 6)), "c": (640, 256, (3, 5)), "d": (896, 128, (4,))}
    tiles = []

    def add_tile(chunks, cols, cost):
        r0 = min(CHUNK[k] for k in chunks) * 256
        c0 = min(groups[c][0] for c in cols)
        nc = sum(groups[c][1] for c in cols)
        deps = sum([xhave[k] for k in chunks], [])
        for c in cols:
            for s in groups[c][2]:
                deps = deps + yhave[s] + [f"c{s}"]
        tiles.append("w" + "".join(map(str, chunks)) + cols)
        g.op(tiles[-1], cost, deps, tile(r0, 256 * len(chunks), c0, nc))

    add_tile((0,), "a", 0.58)
    add_tile((0,), "b", 0.44)
    add_tile((0,), "c", 0.44)
    add_tile((1, 3), "a", 1.0)
    add_tile((1, 3), "b", 0.72)
    add_tile((1, 3), "c", 0.72)
    add_tile((2,), "abcd", 1.3)
    add_tile((0, 1, 3), "d", 0.6)

    def positive(place, h, k, j, xx):
        rc = (Z + C) % 2
        row = pl.multiple_of(place * 256 + h * 128 + j * HALF, HALF)
        s = (4 * C + xx - Z + 8) % 8
        pos = jnp.where(s == 0, 0, jnp.where(s == 4, 7, jnp.where(s < 4, 2 * s - 1, 2 * (8 - s))))
        col = pl.multiple_of(pos * 128, 128)
        yr = pl.multiple_of(pos * 128 + rc * ROWS + h * HALF, HALF)
        xv = xg[pl.ds(row, HALF), :].astype(F32)
        yv = yg[pl.ds(yr, HALF), :].astype(F32)
        z = scale * jnp.sum(xv * yv, axis=1, keepdims=True) + shift
        e = jnp.exp(z)
        wd = (e / (1.0 + e) - 1.0).astype(BF16)
        lane = lax.broadcasted_iota(jnp.int32, (HALF, 128), 1)
        sub = lax.broadcasted_iota(jnp.int32, (HALF, 128), 0)
        hit = lane == sub + rc * ROWS + h * HALF
        old = w[pl.ds(row, HALF), pl.ds(col, 128)]
        w[pl.ds(row, HALF), pl.ds(col, 128)] = jnp.where(hit, wd.astype(F32), old.astype(F32)).astype(BF16)
        zz = jnp.where(hit, z, 0.0)
        lacc[...] -= jnp.sum(zz.reshape(4, 8, 128), axis=0)

    def positives(k):
        def run():
            @pl.when(Y == Z // 2)
            def _():
                positive(CHUNK[k], 1, k, (X - Y + 4) % 4, (X + k) % 4)

                @pl.when((X - Y + 4) % 4 == k)
                def _():
                    for xx in range(4):
                        positive(CHUNK[k], 0, k, (xx - X + 4) % 4, xx)

        return run

    for k in range(4):
        g.op(f"pos{k}", 0.15, [n for n in tiles if str(k) in n], positives(k))
    fixed = [f"pos{k}" for k in range(4)]

    def loss_axis(axis, before):
        n, me, base, kw, lat = {"c": (2, C, 0, "dc", 0.8), "z": (8, Z, 2, "dz", 4.0), "x": (4, X, 10, "dx", 2.6),
                                "y": (4, Y, 14, "dy", 2.6)}[axis]

        def run():
            if before is None:
                v = jnp.full((8, 128), jnp.sum(lacc[...]), F32)
            else:
                b, m = before
                v = lrecv[b]
                for o in range(1, m):
                    v = v + lrecv[b + o]
            lrecv[base + me] = v

        prev = {"c": "", "z": "c", "x": "z", "y": "x"}[axis]
        deps = fixed if axis == "c" else ["l" + prev] + [f"l{prev}{o}" for o in range(1, {"c": 2, "z": 8, "x": 4}[prev])]
        g.op("l" + axis, 0.1, deps, run)
        for o in range(1, n):
            send(f"l{axis}{o}", [], 0, ["l" + axis], lrecv.at[base + me], lrecv.at[base + me], dev(**{kw: o}), "SL", "RL" + axis, lat)

    loss_axis("c", None)
    loss_axis("z", (0, 2))
    loss_axis("x", (2, 8))
    loss_axis("y", (10, 4))

    def loss_end():
        v = lrecv[14]
        for o in range(1, 4):
            v = v + lrecv[14 + o]
        lsum[...] = v
        out_ref[pl.ds(2 * ROWS, 8), pl.ds(0, 128)] = lsum[...] * (1.0 / 16384.0)

    g.op("loss", 0.1, ["ly"] + [f"ly{o}" for o in (1, 2, 3)], loss_end)

    def text(c0, nc):
        def run():
            tf[pl.ds(c0, nc), :] = lax.dot_general(w[:, pl.ds(c0, nc)], xg[...], (((0,), (0,)), ((), ())),
                                                   preferred_element_type=F32)

        return run

    for n, c0, nc, slots in (("4", 896, 128, (4,)), ("35", 640, 256, (3, 5)), ("26", 384, 256, (2, 6)),
                             ("17", 128, 256, (1, 7)), ("0", 0, 128, (0,))):
        g.op("x" + n, 0.06 + 0.52 * nc / 256, fixed, text(c0, nc))
        for s in slots:
            send(f"x{n}c{s}", ["core"], 2 * ROWS, ["x" + n], rows_of(tf, yrow(s, 1), ROWS), rows_of(crecv, s * ROWS, ROWS), dev(dc=1), "SK")

            def add(s=s):
                tf[pl.ds(yrow(s, 0), ROWS), :] += crecv[pl.ds(s * ROWS, ROWS), :]

            g.op(f"k{s}", 0.07, ["x" + n, f"x{n}c{s}"], add)

    slot = 0
    for sign, q in ((1, "p"), (-1, "m")):
        for h in pieces:
            first = 4 if (sign > 0) == (h * PIECE < HALF) else 3
            for t in range(first, 0, -1):
                s = t if sign > 0 else 8 - t
                deps = [f"k{s}"] + ([f"z{q}{t + 1}{h}"] if t < first else [])
                r = slot * PIECE

                def hop(s=s, h=h, r=r, more=t < first):
                    v = tf[pl.ds(yrow(s, 0) + h * PIECE, PIECE), :]
                    if more:
                        v = v + decode(zrecv[pl.ds(r - PIECE, PIECE), :])
                    zsend[pl.ds(r, PIECE), :] = encode(v)

                g.op(f"h{q}{t}{h}", 0.04 + 0.0014 * PIECE, deps, hop)
                send(f"z{q}{t}{h}", ["z+" if sign > 0 else "z-"], PIECE, [f"h{q}{t}{h}"], rows_of(zsend, r, PIECE), rows_of(zrecv, r, PIECE), dev(dz=sign), "SZ")
                slot += 1

            def last(h=h, r=r):
                tf[pl.ds(yrow(0, 0) + h * PIECE, PIECE), :] += decode(zrecv[pl.ds(r, PIECE), :])

            g.op(f"e{q}{h}", 0.06, ["k0", f"z{q}1{h}"], last)

    def text_end():
        out_ref[pl.ds(ROWS, ROWS), :] = scale * tf[pl.ds(yrow(0, 0), ROWS), :]

    g.op("gy", 0.3, [f"e{q}{h}" for q in "pm" for h in pieces], text_end)

    def image(k):
        def run():
            part = jnp.dot(w[pl.ds(CHUNK[k] * 256, 256), :], yg[...], preferred_element_type=F32)
            if k == 2:
                isend[pl.ds(0, 256), :] = encode(part)
                return
            imf[pl.ds(CHUNK[k] * 256, 256), :] = part
            if k:
                for b in (0, 128):
                    o = CHUNK[k] * 256 + b + (64 if k == 1 else 0)
                    isend[pl.ds(o, 64), :] = encode(imf[pl.ds(o, 64), :])

        return run

    for k in (0, 1, 2, 3):
        g.op(f"i{k}", 0.7, [f"pos{k}"], image(k))
    for q, b, ax in (("a", 0, "y"), ("b", 128, "x")):
        def part(name, start, deps, d, b=b, ax=ax, q=q):
            send(name + q, [ax + ("+" if d > 0 else "-")], HALF, deps, rows_of(isend, start + b, HALF), rows_of(irecv, start + b, HALF),
                 dev(**{"d" + ax: d}), "SI")

        ox = "x" if q == "a" else "y"
        for j in (1, 2, 0, 3):
            near, far, d = (1, 3, 1) if j in (0, 1) else (3, 1, -1)
            o2, on, of = j * HALF, CHUNK[near] * 256 + j * HALF, CHUNK[far] * 256 + j * HALF
            part(f"m2{j}", o2, ["i2"], d)
            part(f"m{far}{j}", of, [f"i{far}"], -d)

            def join(on=on, o2=o2, b=b):
                v = imf[pl.ds(on + b, HALF), :] + decode(irecv[pl.ds(o2 + b, HALF), :])
                isend[pl.ds(on + b, HALF), :] = encode(v)

            g.op(f"j{j}{q}", 0.1, [f"i{near}", f"m2{j}{q}"], join)
            part(f"m{near}{j}", on, [f"j{j}{q}"], d)
            r = (2 * (j - 1) + b // 128) * HALF

            def add_up(j=j, b=b, on=on, of=of, r=r):
                v = imf[pl.ds(b + j * HALF, HALF), :] + decode(irecv[pl.ds(on + b, HALF), :]) + decode(irecv[pl.ds(of + b, HALF), :])
                if j:
                    p2send[pl.ds(r, HALF), :] = encode(v)
                else:
                    imf[pl.ds(b, HALF), :] = v

            g.op(f"a{j}{q}", 0.12, ["i0", f"m{near}{j}{q}", f"m{far}{j}{q}"], add_up)
            if j:
                links = {1: [ox + "+"], 2: [ox + "+", ox + "-"], 3: [ox + "-"]}[j]
                send(f"n{j}{q}", links, HALF, [f"a{j}{q}"], rows_of(p2send, r, HALF), rows_of(p2recv, r, HALF), dev(**{"d" + ox: j}), "SN")

                def gather_up(j=j, b=b, r=r):
                    imf[pl.ds(b, HALF), :] += decode(p2recv[pl.ds(r, HALF), :])

                g.op(f"o{j}{q}", 0.07, ["a0" + q, f"n{j}{q}"], gather_up)

    def image_end():
        out_ref[pl.ds(0, HALF), :] = scale * imf[pl.ds(0, HALF), :]
        out_ref[pl.ds(HALF, HALF), :] = scale * imf[pl.ds(128, HALF), :]

    g.op("gx", 0.4, [f"o{j}{q}" for j in (1, 2, 3) for q in "ab"], image_end)
    sizes = {"SY": zsend, "SC": rows_of(xg, 0, 512), "SX": rows_of(xg, 0, 960), "SL": rows_of(lrecv, 0, 14), "SK": crecv, "SZ": zsend,
             "SI": isend, "SN": p2send, "R4": rows_of(xg, 0, 64), "RT": rows_of(xg, 0, 256), "RLc": lrecv.at[0],
             "RLz": rows_of(lrecv, 0, 7), "RLx": rows_of(lrecv, 0, 3), "RLy": rows_of(lrecv, 0, 3)}
    for n, t in g.tasks.items():
        if t["msg"] and t["come"] not in sizes:
            sizes[t["come"]] = rows_of(xg, 0, 64)
    g.emit(ssem, rsem, sizes)


def restore(ref, grads):
    values = ref[...].astype(F32)
    inverse = lax.rsqrt(jnp.sum(values * values, axis=1, keepdims=True) + 1e-06)
    inner = jnp.sum(values * grads, axis=1, keepdims=True)
    return inverse * grads - inverse * inverse * inverse * values * inner


def finish(sums_ref, x_ref, y_ref, loss_ref, gx_ref, gy_ref):
    gx_ref[...] = restore(x_ref, sums_ref[pl.ds(0, ROWS), :])
    gy_ref[...] = restore(y_ref, sums_ref[pl.ds(ROWS, ROWS), :])
    loss_ref[0] = sums_ref[2 * ROWS, 0]


SENT = 8
COME = 117


def local(picture_embeddings, caption_embeddings, sharpness_factor, pairing_shift):
    vmem = pl.BlockSpec(memory_space=pltpu.VMEM)
    smem = pl.BlockSpec(memory_space=pltpu.SMEM)
    sums = pl.pallas_call(
        kernel,
        out_shape=jax.ShapeDtypeStruct((2 * ROWS + 8, D), F32),
        in_specs=[vmem, vmem, smem, smem],
        out_specs=vmem,
        scratch_shapes=[
            pltpu.VMEM((1024, D), BF16),
            pltpu.VMEM((1024, D), BF16),
            pltpu.VMEM((1024, 1024), BF16),
            pltpu.VMEM((768, D), F32),
            pltpu.VMEM((768, D), BF16),
            pltpu.VMEM((768, D), BF16),
            pltpu.VMEM((192, D), BF16),
            pltpu.VMEM((192, D), BF16),
            pltpu.VMEM((1024, D), F32),
            pltpu.VMEM((512, D), F32),
            pltpu.VMEM((448, D), BF16),
            pltpu.VMEM((448, D), BF16),
            pltpu.VMEM((8, 128), F32),
            pltpu.VMEM((8, 128), F32),
            pltpu.VMEM((18, 8, 128), F32),
            pltpu.SemaphoreType.DMA((SENT,)),
            pltpu.SemaphoreType.DMA((COME,)),
        ],
        compiler_params=pltpu.CompilerParams(collective_id=0, has_side_effects=True, vmem_limit_bytes=56 * 2**20),
    )(picture_embeddings, caption_embeddings, sharpness_factor, pairing_shift)
    return pl.pallas_call(
        finish,
        out_shape=(
            jax.ShapeDtypeStruct((1,), F32),
            jax.ShapeDtypeStruct((ROWS, D), F32),
            jax.ShapeDtypeStruct((ROWS, D), F32),
        ),
        in_specs=[vmem, vmem, vmem],
        out_specs=(smem, vmem, vmem),
    )(sums, picture_embeddings, caption_embeddings)


def solution(mesh):
    in_specs = (P(("img", "txt"), None), P(("txt", "img"), None), P(), P())
    out_specs = (P(), P(("img", "txt"), None), P(("txt", "img"), None))
    return jax.shard_map(local, mesh=mesh, in_specs=in_specs, out_specs=out_specs, check_vma=False)
```

time: 421 us -> 56.1 us (0.13)
  waiting for transfers between devices: 286 us -> 0 us
  blocking collectives: 78.3 us -> 0 us
  Pallas kernels: 0 us -> 53.9 us
  matrix products: 23.2 us -> 0 us
  between operations: 16.9 us -> 2.09 us
  other arithmetic: 11.2 us -> 0 us
    reduce_scatter x2 -> x0, waiting for transfers between devices: 175 us -> none  [the longest x1 175 us: local(): gxn = lax.psum_scatter(image_part, 'txt', scatter_dimension=0, tiled=True)]
    all_gather x2 -> x0, waiting for transfers between devices: 110 us -> none  [the longest x1 83.6 us: local(): x_block = lax.all_gather(xn, 'txt', axis=0, tiled=True)]
    psum x1 -> x0, blocking collectives: 78.3 us -> none  [local(): total = lax.psum(partial_loss_value, ('img', 'txt'))]
    pallas_call x0 -> x2, Pallas kernels: none -> 53.9 us  [the longest x1 51.7 us: local(): pl.pallas_call(kernel, out_shape=jax.ShapeDtypeStruct((2 * ROWS + 8, D),...]
    dot_general x3 -> x0, matrix products: 23.2 us -> none  [the longest x1 9.63 us: local(): jnp.dot(weight, y_block, preferred_element_type=jnp.float32)]
    reduce_sum x4 -> x0, other arithmetic: 4.27 us -> none  [the longest x2 2.19 us: restore(): inner = jnp.sum(values * grads, axis=1, keepdims=True)]
  transfers between devices with their start and end apart: 4 -> 0, of which waited for: 3 -> 0; matrix products, arithmetic and copies ran while one was open for 4% -> 0% of each run, Pallas kernels for 0% -> 0%
where the time goes in v2:
time: 56.1 us; the launch traced here: 56 us
  Pallas kernels  53.9 us (96%)
  between operations  2.09 us (4%)
    pallas_call x1, Pallas kernels, local(): pl.pallas_call(kernel, out_shape=jax.ShapeDtypeStruct((2 * ROWS + 8, D),...  51.7 us
    pallas_call x1, Pallas kernels, local(): pl.pallas_call(finish, out_shape=(jax.ShapeDtypeStruct((1,), F32), jax.Sh...  2.2 us

profile of v2, /device:TPU:1, one launch (start us, length us, event | category | flops | bytes accessed | tf_op | source)
XLA Modules:
  0.0 56.0 jit_solution(3444487899376932393)
XLA Ops:
  1.9 51.7 %shard_map.67.sums_ref = f32[136,1152]{1,0:T(8,128)} custom-call(bf16[64,1152]{1,0:T(8,128)(2,1)} %x_ref.3, bf16[64,1152]{1,0:T(8,128)(2,1)} %y_ref.3, f32[1]{0:T(128)S(6)} %copy.7.scale_ref, f32[1]{0:T(128)S(6)} %copy.8.shift_ref), custom_call_target="tpu_custom_call" | custom-call | tf_op jit(solution)/shard_map/pallas_call | solution.py:494
  53.6 2.2 %shard_map.68 = (f32[1]{0:T(128)}, f32[64,1152]{1,0:T(8,128)}, f32[64,1152]{1,0:T(8,128)}) custom-call(f32[136,1152]{1,0:T(8,128)} %shard_map.67.sums_ref, bf16[64,1152]{1,0:T(8,128)(2,1)} %x_ref.3, bf16[64,1152]{1,0:T(8,128)(2,1)} %y_ref.3), custom_call_target="tpu_custom_call" | custom-call | tf_op jit(solution)/shard_map/pallas_call | solution.py:520

commit v3 on v2

--- a/solution.py
+++ b/solution.py
@@ -145,9 +145,16 @@
     return jnp.where(p < 0.01, small, jnp.log(1.0 + p))
 
 
-def kernel(x_ref, y_ref, scale_ref, shift_ref, out_ref,
+def restore(raw, grads):
+    values = raw.astype(F32)
+    inverse = lax.rsqrt(jnp.sum(values * values, axis=1, keepdims=True) + 1e-06)
+    inner = jnp.sum(values * grads, axis=1, keepdims=True)
+    return inverse * grads - inverse * inverse * inverse * values * inner
+
+
+def kernel(x_hbm, y_hbm, scale_hbm, shift_hbm, out_ref,
            xg, yg, w, imf, isend, irecv, p2send, p2recv, tf, crecv, zsend, zrecv,
-           lacc, lsum, lrecv, ssem, rsem):
+           lacc, lsum, lrecv, x_ref, y_ref, scale_ref, shift_ref, csem, ssem, rsem):
     img, txt = lax.axis_index("img"), lax.axis_index("txt")
     Y, C = img // 2, img % 2
     X, Z = txt // 8, txt % 8
@@ -155,8 +162,12 @@
     def dev(dx=0, dy=0, dz=0, dc=0):
         return (((Y + dy) % 4) * 2 + (C + dc) % 2, ((X + dx) % 4) * 8 + (Z + dz) % 8)
 
+    inputs = [pltpu.make_async_copy(a, b, csem.at[i]) for i, (a, b) in enumerate(
+        ((y_hbm, y_ref), (x_hbm, x_ref), (scale_hbm, scale_ref), (shift_hbm, shift_ref)))]
+    for c in inputs:
+        c.start()
     barrier = pltpu.get_barrier_semaphore()
-    peers = ([dev(dz=i) for i in range(1, 8)] + [dev(dx=i) for i in (1, 2, 3)] + [dev(dy=i) for i in (1, 2, 3)]
+    peers = ([dev(dz=1), dev(dz=-1)] + [dev(dx=i) for i in (1, 2, 3)] + [dev(dy=i) for i in (1, 2, 3)]
              + [dev(dc=1)])
     for p in peers:
         pl.semaphore_signal(barrier, inc=1, device_id=p, device_id_type=MESH)
@@ -175,26 +186,27 @@
     def yrow(s, rc):
         return POS[s] * 128 + rc * ROWS
 
-    scale = scale_ref[0]
-    shift = shift_ref[0]
-
     g = Schedule()
 
     def send(name, links, rows, deps, src, dst, to, sent, come=None, lat=None):
         if lat is None:
-            lat = LATENCY["core"] if links == ["core"] else LATENCY[len(links)]
+            lat = LATENCY["core"] if links == ["core"] else LATENCY[max(1, len(links))]
         g.msg(name, links, rows, lat, deps, lambda ss, rs: pltpu.make_async_remote_copy(
             src_ref=src, dst_ref=dst, send_sem=ss, recv_sem=rs, device_id=to, device_id_type=MESH), sent, come or name)
 
     def own_text():
+        inputs[0].wait()
         yg[pl.ds(yrow(0, 0), ROWS)] = unit(y_ref)
         pl.semaphore_wait(barrier, len(peers))
 
     def own_image():
+        inputs[1].wait()
         xn = unit(x_ref)
         xg[pl.ds(A(0, 0), HALF)] = xn[:HALF]
         xg[pl.ds(B(0, 0), HALF)] = xn[HALF:]
         lacc[...] = jnp.zeros_like(lacc)
+        for c in inputs[2:]:
+            c.wait()
 
     g.op("ny", 0.3, [], own_text)
     g.op("nx", 0.3, ["ny"], own_image)
@@ -243,7 +255,7 @@
         def run():
             dots = lax.dot_general(xg[pl.ds(r0, nr), :], yg[pl.ds(c0, nc), :], (((1,), (1,)), ((), ())),
                                    preferred_element_type=F32)
-            e = jnp.exp2(dots * (scale * LOG2E) + shift * LOG2E)
+            e = jnp.exp2(dots * (scale_ref[0] * LOG2E) + shift_ref[0] * LOG2E)
             d = 1.0 + e
             r = pl.reciprocal(d, approx=True)
             r = r * (2.0 - d * r)
@@ -295,7 +307,7 @@
         yr = pl.multiple_of(pos * 128 + rc * ROWS + h * HALF, HALF)
         xv = xg[pl.ds(row, HALF), :].astype(F32)
         yv = yg[pl.ds(yr, HALF), :].astype(F32)
-        z = scale * jnp.sum(xv * yv, axis=1, keepdims=True) + shift
+        z = scale_ref[0] * jnp.sum(xv * yv, axis=1, keepdims=True) + shift_ref[0]
         e = jnp.exp(z)
         wd = (e / (1.0 + e) - 1.0).astype(BF16)
         lane = lax.broadcasted_iota(jnp.int32, (HALF, 128), 1)
@@ -338,8 +350,15 @@
             lrecv[base + me] = v
 
         prev = {"c": "", "z": "c", "x": "z", "y": "x"}[axis]
-        deps = fixed if axis == "c" else ["l" + prev] + [f"l{prev}{o}" for o in range(1, {"c": 2, "z": 8, "x": 4}[prev])]
+        hops = ("zu1", "zu2", "zu3", "zu4", "zd1", "zd2", "zd3")
+        deps = fixed if axis == "c" else ["l" + prev] + ([f"l{q}" for q in hops] if prev == "z" else [f"l{prev}{o}" for o in range(1, {"c": 2, "x": 4}[prev])])
         g.op("l" + axis, 0.1, deps, run)
+        if axis == "z":
+            for q, sign, far in (("u", 1, 4), ("d", -1, 3)):
+                for t in range(1, far + 1):
+                    at = base + (Z - sign * (t - 1) + 8) % 8
+                    send(f"lz{q}{t}", [], 0, [f"lz{q}{t - 1}" if t > 1 else "lz"], lrecv.at[at], lrecv.at[at], dev(dz=sign), "SL")
+            return
         for o in range(1, n):
             send(f"l{axis}{o}", [], 0, ["l" + axis], lrecv.at[base + me], lrecv.at[base + me], dev(**{kw: o}), "SL", "RL" + axis, lat)
 
@@ -400,7 +419,7 @@
             g.op(f"e{q}{h}", 0.06, ["k0", f"z{q}1{h}"], last)
 
     def text_end():
-        out_ref[pl.ds(ROWS, ROWS), :] = scale * tf[pl.ds(yrow(0, 0), ROWS), :]
+        out_ref[pl.ds(ROWS, ROWS), :] = restore(y_ref[...], scale_ref[0] * tf[pl.ds(yrow(0, 0), ROWS), :])
 
     g.op("gy", 0.3, [f"e{q}{h}" for q in "pm" for h in pieces], text_end)
 
@@ -458,8 +477,8 @@
                 g.op(f"o{j}{q}", 0.07, ["a0" + q, f"n{j}{q}"], gather_up)
 
     def image_end():
-        out_ref[pl.ds(0, HALF), :] = scale * imf[pl.ds(0, HALF), :]
-        out_ref[pl.ds(HALF, HALF), :] = scale * imf[pl.ds(128, HALF), :]
+        for o, b in ((0, 0), (HALF, 128)):
+            out_ref[pl.ds(o, HALF), :] = restore(x_ref[pl.ds(o, HALF), :], scale_ref[0] * imf[pl.ds(b, HALF), :])
 
     g.op("gx", 0.4, [f"o{j}{q}" for j in (1, 2, 3) for q in "ab"], image_end)
     sizes = {"SY": zsend, "SC": rows_of(xg, 0, 512), "SX": rows_of(xg, 0, 960), "SL": rows_of(lrecv, 0, 14), "SK": crecv, "SZ": zsend,
@@ -471,30 +490,24 @@
     g.emit(ssem, rsem, sizes)
 
 
-def restore(ref, grads):
-    values = ref[...].astype(F32)
-    inverse = lax.rsqrt(jnp.sum(values * values, axis=1, keepdims=True) + 1e-06)
-    inner = jnp.sum(values * grads, axis=1, keepdims=True)
-    return inverse * grads - inverse * inverse * inverse * values * inner
-
-
-def finish(sums_ref, x_ref, y_ref, loss_ref, gx_ref, gy_ref):
-    gx_ref[...] = restore(x_ref, sums_ref[pl.ds(0, ROWS), :])
-    gy_ref[...] = restore(y_ref, sums_ref[pl.ds(ROWS, ROWS), :])
-    loss_ref[0] = sums_ref[2 * ROWS, 0]
+def finish(grads_ref, loss_ref, gx_ref, gy_ref):
+    gx_ref[...] = grads_ref[pl.ds(0, ROWS), :]
+    gy_ref[...] = grads_ref[pl.ds(ROWS, ROWS), :]
+    loss_ref[0] = grads_ref[2 * ROWS, 0]
 
 
 SENT = 8
-COME = 117
+COME = 123
 
 
 def local(picture_embeddings, caption_embeddings, sharpness_factor, pairing_shift):
     vmem = pl.BlockSpec(memory_space=pltpu.VMEM)
     smem = pl.BlockSpec(memory_space=pltpu.SMEM)
-    sums = pl.pallas_call(
+    hbm = pl.BlockSpec(memory_space=pltpu.HBM)
+    grads = pl.pallas_call(
         kernel,
         out_shape=jax.ShapeDtypeStruct((2 * ROWS + 8, D), F32),
-        in_specs=[vmem, vmem, smem, smem],
+        in_specs=[hbm, hbm, hbm, hbm],
         out_specs=vmem,
         scratch_shapes=[
             pltpu.VMEM((1024, D), BF16),
@@ -512,10 +525,15 @@
             pltpu.VMEM((8, 128), F32),
             pltpu.VMEM((8, 128), F32),
             pltpu.VMEM((18, 8, 128), F32),
+            pltpu.VMEM((ROWS, D), BF16),
+            pltpu.VMEM((ROWS, D), BF16),
+            pltpu.SMEM((1,), F32),
+            pltpu.SMEM((1,), F32),
+            pltpu.SemaphoreType.DMA((4,)),
             pltpu.SemaphoreType.DMA((SENT,)),
             pltpu.SemaphoreType.DMA((COME,)),
         ],
-        compiler_params=pltpu.CompilerParams(collective_id=0, has_side_effects=True, vmem_limit_bytes=56 * 2**20),
+        compiler_params=pltpu.CompilerParams(collective_id=0, has_side_effects=True, vmem_limit_bytes=40 * 2**20),
     )(picture_embeddings, caption_embeddings, sharpness_factor, pairing_shift)
     return pl.pallas_call(
         finish,
@@ -524,9 +542,10 @@
             jax.ShapeDtypeStruct((ROWS, D), F32),
             jax.ShapeDtypeStruct((ROWS, D), F32),
         ),
-        in_specs=[vmem, vmem, vmem],
+        in_specs=[vmem],
         out_specs=(smem, vmem, vmem),
-    )(sums, picture_embeddings, caption_embeddings)
+        compiler_params=pltpu.CompilerParams(vmem_limit_bytes=4 * 2**20),
+    )(grads)
 
 
 def solution(mesh):

time: 56.1 us -> 54.7 us (0.975)
  Pallas kernels: 53.9 us -> 50.4 us
  local copies, waits for them, and re-layouts: 0 us -> 1.81 us
    pallas_call x1, Pallas kernels: 51.7 us -> 49.5 us  [local(): pl.pallas_call(kernel, out_shape=jax.ShapeDtypeStruct((2 * ROWS + 8, D),...]
    unnamed x0 -> x4, local copies, waits for them, and re-layouts: none -> 1.81 us
    pallas_call x1, Pallas kernels: 2.2 us -> 0.84 us  [local(): pl.pallas_call(finish, out_shape=(jax.ShapeDtypeStruct((1,), F32), jax.Sh...]
where the time goes in v3:
time: 54.7 us; the launch traced here: 54.3 us
  Pallas kernels  50.4 us (92%)
  between operations  2.1 us (4%)
  local copies, waits for them, and re-layouts  1.81 us (3%)
    pallas_call x1, Pallas kernels, local(): pl.pallas_call(kernel, out_shape=jax.ShapeDtypeStruct((2 * ROWS + 8, D),...  49.5 us
    unnamed x4, local copies, waits for them, and re-layouts  1.81 us

profile of v3, /device:TPU:1, one launch (start us, length us, event | category | flops | bytes accessed | tf_op | source)
XLA Modules:
  0.0 54.3 jit_solution(6927451473067204525)
XLA Ops:
  1.9 0.0 copy-start
  1.9 0.9 %copy-done = bf16[64,1152]{1,0:T(8,128)(2,1)S(1)} copy-done((bf16[64,1152]{1,0:T(8,128)(2,1)S(1)}, bf16[64,1152]{1,0:T(8,128)(2,1)}, u32[]{:S(2)}) %copy-start) | copy-done | bytes 147480
  2.8 0.0 copy-start.1
  2.8 0.9 %copy-done.1 = bf16[64,1152]{1,0:T(8,128)(2,1)S(1)} copy-done((bf16[64,1152]{1,0:T(8,128)(2,1)S(1)}, bf16[64,1152]{1,0:T(8,128)(2,1)}, u32[]{:S(2)}) %copy-start.1) | copy-done | bytes 147480
  3.7 49.5 %shard_map.67.grads_ref = f32[136,1152]{1,0:T(8,128)S(1)} custom-call(bf16[64,1152]{1,0:T(8,128)(2,1)S(1)} %copy-done, bf16[64,1152]{1,0:T(8,128)(2,1)S(1)} %copy-done.1, f32[1]{0:T(128)S(6)} %copy.7.scale_hbm, f32[1]{0:T(128)S(6)} %copy.8.shift_hbm), custom_call_target="tpu_custom_call" | custom-call | tf_op jit(solution)/shard_map/pallas_call | solution.py:507
  53.3 0.8 %shard_map.68 = (f32[1]{0:T(128)}, f32[64,1152]{1,0:T(8,128)}, f32[64,1152]{1,0:T(8,128)}) custom-call(f32[136,1152]{1,0:T(8,128)S(1)} %shard_map.67.grads_ref), custom_call_target="tpu_custom_call" | custom-call | tf_op jit(solution)/shard_map/pallas_call | solution.py:538
Async XLA Ops:
  1.9 0.9 %copy-start = (bf16[64,1152]{1,0:T(8,128)(2,1)S(1)}, bf16[64,1152]{1,0:T(8,128)(2,1)}, u32[]{:S(2)}) copy-start(bf16[64,1152]{1,0:T(8,128)(2,1)} %x_hbm.1) | copy-start | bytes 442372
  2.8 0.9 %copy-start.1 = (bf16[64,1152]{1,0:T(8,128)(2,1)S(1)}, bf16[64,1152]{1,0:T(8,128)(2,1)}, u32[]{:S(2)}) copy-start(bf16[64,1152]{1,0:T(8,128)(2,1)} %y_hbm.1) | copy-start | bytes 442372

commit v4 on v3

--- a/solution.py
+++ b/solution.py
@@ -17,7 +17,7 @@
 CHUNK = {0: 0, 1: 1, 3: 2, 2: 3}
 RATE = {"core": 300.0}
 LINK_RATE = 20.6
-LATENCY = {"core": 0.8, 1: 2.0, 2: 2.7}
+LATENCY = {"core": 1.0, 1: 2.2, 2: 3.0}
 BACKLOG = 1.6
 ISSUE = 0.03
 WAIT = 0.015
@@ -298,42 +298,38 @@
     add_tile((2,), "abcd", 1.3)
     add_tile((0, 1, 3), "d", 0.6)
 
-    def positive(place, h, k, j, xx):
-        rc = (Z + C) % 2
-        row = pl.multiple_of(place * 256 + h * 128 + j * HALF, HALF)
-        s = (4 * C + xx - Z + 8) % 8
-        pos = jnp.where(s == 0, 0, jnp.where(s == 4, 7, jnp.where(s < 4, 2 * s - 1, 2 * (8 - s))))
-        col = pl.multiple_of(pos * 128, 128)
-        yr = pl.multiple_of(pos * 128 + rc * ROWS + h * HALF, HALF)
-        xv = xg[pl.ds(row, HALF), :].astype(F32)
-        yv = yg[pl.ds(yr, HALF), :].astype(F32)
-        z = scale_ref[0] * jnp.sum(xv * yv, axis=1, keepdims=True) + shift_ref[0]
-        e = jnp.exp(z)
-        wd = (e / (1.0 + e) - 1.0).astype(BF16)
-        lane = lax.broadcasted_iota(jnp.int32, (HALF, 128), 1)
-        sub = lax.broadcasted_iota(jnp.int32, (HALF, 128), 0)
-        hit = lane == sub + rc * ROWS + h * HALF
-        old = w[pl.ds(row, HALF), pl.ds(col, 128)]
-        w[pl.ds(row, HALF), pl.ds(col, 128)] = jnp.where(hit, wd.astype(F32), old.astype(F32)).astype(BF16)
-        zz = jnp.where(hit, z, 0.0)
-        lacc[...] -= jnp.sum(zz.reshape(4, 8, 128), axis=0)
-
-    def positives(k):
-        def run():
-            @pl.when(Y == Z // 2)
-            def _():
-                positive(CHUNK[k], 1, k, (X - Y + 4) % 4, (X + k) % 4)
-
-                @pl.when((X - Y + 4) % 4 == k)
-                def _():
-                    for xx in range(4):
-                        positive(CHUNK[k], 0, k, (xx - X + 4) % 4, xx)
-
-        return run
-
-    for k in range(4):
-        g.op(f"pos{k}", 0.15, [n for n in tiles if str(k) in n], positives(k))
-    fixed = [f"pos{k}" for k in range(4)]
+    def positives():
+        @pl.when(Y == Z // 2)
+        def _():
+            rc = (Z + C) % 2
+            blocks = []
+            for xx in range(4):
+                for h in (0, 1):
+                    k, j = (X - Y + 4) % 4, (xx - X + 4) % 4
+                    if h == 1:
+                        k, j = j, k
+                    row = pl.multiple_of(jnp.where(k < 2, k, 5 - k) * 256 + h * 128 + j * HALF, HALF)
+                    s = (4 * C + xx - Z + 8) % 8
+                    pos = jnp.where(s == 0, 0, jnp.where(s == 4, 7, jnp.where(s < 4, 2 * s - 1, 2 * (8 - s))))
+                    col = pl.multiple_of(pos * 128, 128)
+                    yr = pl.multiple_of(pos * 128 + rc * ROWS + h * HALF, HALF)
+                    xv = xg[pl.ds(row, HALF), :].astype(F32)
+                    yv = yg[pl.ds(yr, HALF), :].astype(F32)
+                    z = scale_ref[0] * jnp.sum(xv * yv, axis=1, keepdims=True) + shift_ref[0]
+                    blocks.append((row, col, h, z, w[pl.ds(row, HALF), pl.ds(col, 128)]))
+            less = jnp.zeros((8, 128), F32)
+            lane = lax.broadcasted_iota(jnp.int32, (HALF, 128), 1)
+            sub = lax.broadcasted_iota(jnp.int32, (HALF, 128), 0)
+            for row, col, h, z, old in blocks:
+                e = jnp.exp(z)
+                wd = (e / (1.0 + e) - 1.0).astype(BF16)
+                hit = lane == sub + rc * ROWS + h * HALF
+                w[pl.ds(row, HALF), pl.ds(col, 128)] = jnp.where(hit, wd.astype(F32), old.astype(F32)).astype(BF16)
+                less += jnp.sum(jnp.where(hit, z, 0.0).reshape(4, 8, 128), axis=0)
+            lacc[...] -= less
+
+    g.op("pos", 0.4, tiles, positives)
+    fixed = ["pos"]
 
     def loss_axis(axis, before):
         n, me, base, kw, lat = {"c": (2, C, 0, "dc", 0.8), "z": (8, Z, 2, "dz", 4.0), "x": (4, X, 10, "dx", 2.6),
@@ -438,7 +434,7 @@
         return run
 
     for k in (0, 1, 2, 3):
-        g.op(f"i{k}", 0.7, [f"pos{k}"], image(k))
+        g.op(f"i{k}", 0.7, ["pos"], image(k))
     for q, b, ax in (("a", 0, "y"), ("b", 128, "x")):
         def part(name, start, deps, d, b=b, ax=ax, q=q):
             send(name + q, [ax + ("+" if d > 0 else "-")], HALF, deps, rows_of(isend, start + b, HALF), rows_of(irecv, start + b, HALF),

time: 54.7 us -> 53.9 us (0.985)
  Pallas kernels: 50.4 us -> 49.6 us
    pallas_call x1, Pallas kernels: 49.5 us -> 48.8 us  [local(): pl.pallas_call(kernel, out_shape=jax.ShapeDtypeStruct((2 * ROWS + 8, D),...]
where the time goes in v4:
time: 53.9 us; the launch traced here: 53.5 us
  Pallas kernels  49.6 us (92%)
  between operations  2.1 us (4%)
  local copies, waits for them, and re-layouts  1.81 us (3%)
    pallas_call x1, Pallas kernels, local(): pl.pallas_call(kernel, out_shape=jax.ShapeDtypeStruct((2 * ROWS + 8, D),...  48.8 us
    unnamed x4, local copies, waits for them, and re-layouts  1.81 us

profile of v4, /device:TPU:1, one launch (start us, length us, event | category | flops | bytes accessed | tf_op | source)
XLA Modules:
  0.0 53.5 jit_solution(1683996877794381121)
XLA Ops:
  1.9 0.0 copy-start
  1.9 0.9 %copy-done = bf16[64,1152]{1,0:T(8,128)(2,1)S(1)} copy-done((bf16[64,1152]{1,0:T(8,128)(2,1)S(1)}, bf16[64,1152]{1,0:T(8,128)(2,1)}, u32[]{:S(2)}) %copy-start) | copy-done | bytes 147480
  2.8 0.0 copy-start.1
  2.8 0.9 %copy-done.1 = bf16[64,1152]{1,0:T(8,128)(2,1)S(1)} copy-done((bf16[64,1152]{1,0:T(8,128)(2,1)S(1)}, bf16[64,1152]{1,0:T(8,128)(2,1)}, u32[]{:S(2)}) %copy-start.1) | copy-done | bytes 147480
  3.7 48.8 %shard_map.67.grads_ref = f32[136,1152]{1,0:T(8,128)S(1)} custom-call(bf16[64,1152]{1,0:T(8,128)(2,1)S(1)} %copy-done, bf16[64,1152]{1,0:T(8,128)(2,1)S(1)} %copy-done.1, f32[1]{0:T(128)S(6)} %copy.7.scale_hbm, f32[1]{0:T(128)S(6)} %copy.8.shift_hbm), custom_call_target="tpu_custom_call" | custom-call | tf_op jit(solution)/shard_map/pallas_call | solution.py:503
  52.5 0.8 %shard_map.68 = (f32[1]{0:T(128)}, f32[64,1152]{1,0:T(8,128)}, f32[64,1152]{1,0:T(8,128)}) custom-call(f32[136,1152]{1,0:T(8,128)S(1)} %shard_map.67.grads_ref), custom_call_target="tpu_custom_call" | custom-call | tf_op jit(solution)/shard_map/pallas_call | solution.py:534
Async XLA Ops:
  1.9 0.9 %copy-start = (bf16[64,1152]{1,0:T(8,128)(2,1)S(1)}, bf16[64,1152]{1,0:T(8,128)(2,1)}, u32[]{:S(2)}) copy-start(bf16[64,1152]{1,0:T(8,128)(2,1)} %x_hbm.1) | copy-start | bytes 442372
  2.8 0.9 %copy-start.1 = (bf16[64,1152]{1,0:T(8,128)(2,1)S(1)}, bf16[64,1152]{1,0:T(8,128)(2,1)}, u32[]{:S(2)}) copy-start(bf16[64,1152]{1,0:T(8,128)(2,1)} %y_hbm.1) | copy-start | bytes 442372

commit v5 on v4

--- a/solution.py
+++ b/solution.py
@@ -71,7 +71,7 @@
             if not ready:
                 now = min(later)
                 continue
-            n = max(ready, key=lambda n: (self.tasks[n]["msg"], level[n]))
+            n = max(ready, key=lambda n: (self.tasks[n]["msg"], n[0] == "l", level[n]))
             left.remove(n)
             out.append(n)
             t = self.tasks[n]

time: 53.9 us -> 53.9 us (level)
  no operation moved by 1% of the time
where the time goes in v5:
time: 53.9 us; the launch traced here: 53.5 us
  Pallas kernels  49.6 us (92%)
  between operations  2.1 us (4%)
  local copies, waits for them, and re-layouts  1.81 us (3%)
    pallas_call x1, Pallas kernels, local(): pl.pallas_call(kernel, out_shape=jax.ShapeDtypeStruct((2 * ROWS + 8, D),...  48.8 us
    unnamed x4, local copies, waits for them, and re-layouts  1.81 us

profile of v5, /device:TPU:1, one launch (start us, length us, event | category | flops | bytes accessed | tf_op | source)
XLA Modules:
  0.0 53.5 jit_solution(5989547794863901999)
XLA Ops:
  1.9 0.0 copy-start
  1.9 0.9 %copy-done = bf16[64,1152]{1,0:T(8,128)(2,1)S(1)} copy-done((bf16[64,1152]{1,0:T(8,128)(2,1)S(1)}, bf16[64,1152]{1,0:T(8,128)(2,1)}, u32[]{:S(2)}) %copy-start) | copy-done | bytes 147480
  2.8 0.0 copy-start.1
  2.8 0.9 %copy-done.1 = bf16[64,1152]{1,0:T(8,128)(2,1)S(1)} copy-done((bf16[64,1152]{1,0:T(8,128)(2,1)S(1)}, bf16[64,1152]{1,0:T(8,128)(2,1)}, u32[]{:S(2)}) %copy-start.1) | copy-done | bytes 147480
  3.7 48.8 %shard_map.67.grads_ref = f32[136,1152]{1,0:T(8,128)S(1)} custom-call(bf16[64,1152]{1,0:T(8,128)(2,1)S(1)} %copy-done, bf16[64,1152]{1,0:T(8,128)(2,1)S(1)} %copy-done.1, f32[1]{0:T(128)S(6)} %copy.7.scale_hbm, f32[1]{0:T(128)S(6)} %copy.8.shift_hbm), custom_call_target="tpu_custom_call" | custom-call | tf_op jit(solution)/shard_map/pallas_call | solution.py:503
  52.5 0.8 %shard_map.68 = (f32[1]{0:T(128)}, f32[64,1152]{1,0:T(8,128)}, f32[64,1152]{1,0:T(8,128)}) custom-call(f32[136,1152]{1,0:T(8,128)S(1)} %shard_map.67.grads_ref), custom_call_target="tpu_custom_call" | custom-call | tf_op jit(solution)/shard_map/pallas_call | solution.py:534
Async XLA Ops:
  1.9 0.9 %copy-start = (bf16[64,1152]{1,0:T(8,128)(2,1)S(1)}, bf16[64,1152]{1,0:T(8,128)(2,1)}, u32[]{:S(2)}) copy-start(bf16[64,1152]{1,0:T(8,128)(2,1)} %x_hbm.1) | copy-start | bytes 442372
  2.8 0.9 %copy-start.1 = (bf16[64,1152]{1,0:T(8,128)(2,1)S(1)}, bf16[64,1152]{1,0:T(8,128)(2,1)}, u32[]{:S(2)}) copy-start(bf16[64,1152]{1,0:T(8,128)(2,1)} %y_hbm.1) | copy-start | bytes 442372
